TPU v7x, 32 devices: a whole 2x2x4 slice. The times are simulated.
32 devices in a mesh: grp: 4 (over z), tile: 8 (over y, x, core).
Axes of the slice: x: 2, y: 2, z: 4, core: 2. Of those that a mesh axis runs over, the one named last changes fastest.
Arguments:
- latent: float32 [512, 128], P(('grp', 'tile')), may hold values from -6 to 6
- momentum: float32 [512, 128], P(('grp', 'tile')), may hold values from -6 to 6
- observed: float32 [512, 128], P(('grp', 'tile')), may hold values from -8 to 8
- nugget: float32 [512, 128], P(('grp', 'tile')), may hold values from 0.25 to 2
- cond_weights: float32 [512, 128, 256], P(('grp', 'tile')), may hold values from -0.375 to 0.375
- whiten: float32 [512, 128, 128], P(('grp', 'tile')), may hold values from -4 to 4
- slot_of_rank: int32 [512], replicated, may hold values from 0 to 511, as said below
- neighbours: int32 [512, 2], P(('grp', 'tile')), may hold values from 0 to 479, as said below
Outputs:
- moved: float32 [512, 128], P(('grp', 'tile'))
- new_momentum: float32 [512, 128], P(('grp', 'tile'))
Inputs may be any that keep to these rules, and one draw needn't show every extreme that they name: `slot_of_rank`: A permutation of the 512 slots; slot s is place s % 16 of device s // 16 in the order of grp then tile. Ranks below 64 are coarse blocks: each device holds exactly 2 of them, in its first 2 places. `neighbours`: both entries are distinct ranks lower than the block's own, except that the block of rank 0 lists 0 twice and the block of rank 1 lists 0 and 1; an entry equal to the block's own rank counts as absent. The first entry is always a coarse rank; the second is a coarse rank or the rank of a block held by the same device or by the device one tile index lower or higher in the same group. The block of rank 512 - 1 names rank 512 - 33 as its second entry.
All inputs are finite; a program needn't handle non-finite values.
Results may differ from a plain program's by a relative error of at most 0.00009.
Values sent between devices are 32-bit elements; how exact they have to be, the bound alone decides.
A program may use at most 64 MiB of HBM per device.

v0:
```python
import jax
import jax.numpy as jnp
from jax import lax
from jax.sharding import PartitionSpec as P

COARSE_DEV = 2


leap_step = 0.25


def with_halo(x, sides, width):
    for axis, dim in sides:
        devices, length = (lax.axis_size(axis), x.shape[dim])
        up = [(i, (i + 1) % devices) for i in range(devices - 1)]
        down = [(j, i) for i, j in up]
        last = lax.slice_in_dim(x, length - width, length, axis=dim)
        leading = lax.slice_in_dim(x, 0, width, axis=dim)
        before = lax.ppermute(last, axis, up)
        after = lax.ppermute(leading, axis, down)
        x = jnp.concatenate([before, x, after], axis=dim)
    return x


def shifted(value, axis, steps):
    count = lax.axis_size(axis)
    leading, last = (max(0, -steps), min(count, count - steps))
    return lax.ppermute(value, axis, [(source, source + steps) for source in range(leading, last)])


def on_device(latent, momentum, observed, nugget, cond_weights, whiten, slot_of_rank, neighbours):
    blocks = latent.shape[0]
    total = slot_of_rank.shape[0]
    device = lax.axis_index(("grp", "tile"))
    ncoarse = COARSE_DEV * lax.axis_size(("grp", "tile"))
    local_slots = device * blocks + jnp.arange(blocks, dtype=jnp.int32)
    all_ranks = jnp.arange(total, dtype=jnp.int32)
    own_rank = jnp.sum(
        jnp.where(slot_of_rank[None, :] == local_slots[:, None], all_ranks[None, :], 0), axis=1
    )
    present = (neighbours != own_rank[:, None]).astype(jnp.float32)
    cond_slots = slot_of_rank[neighbours]
    owner_dev = cond_slots // blocks
    local_place = cond_slots % blocks
    coarse_row = owner_dev * COARSE_DEV + local_place
    near_row = ncoarse + (owner_dev - device + 1) * blocks + local_place
    lookup_index = jnp.where(neighbours < ncoarse, coarse_row, near_row)
    flat_index = lookup_index.reshape(-1)

    def gradient(latent_now):
        coarse_table = lax.all_gather(latent_now[:COARSE_DEV], ("grp", "tile"), axis=0, tiled=True)
        beside_all = with_halo(latent_now, (("tile", 0),), blocks)
        lookup = jnp.concatenate([coarse_table, beside_all], axis=0)
        cond_values = (lookup[lookup_index] * present[:, :, None]).reshape(blocks, -1)
        cond_mean = jnp.einsum(
            "bij,bj->bi", cond_weights, cond_values, precision=lax.Precision.HIGHEST
        )
        whitened = jnp.einsum(
            "bij,bj->bi", whiten, latent_now - cond_mean, precision=lax.Precision.HIGHEST
        )
        own_term = jnp.einsum("bji,bj->bi", whiten, whitened, precision=lax.Precision.HIGHEST)
        push_back = jnp.einsum(
            "bji,bj->bi", cond_weights, own_term, precision=lax.Precision.HIGHEST
        )
        push_back = push_back.reshape(blocks, 2, -1) * present[:, :, None]
        pulled = jnp.zeros((lookup.shape[0], latent_now.shape[1]), jnp.float32)
        pulled = pulled.at[flat_index].add(push_back.reshape(blocks * 2, -1))
        coarse_part = pulled[:ncoarse]
        lower = pulled[ncoarse : ncoarse + blocks]
        middle = pulled[ncoarse + blocks : ncoarse + 2 * blocks]
        upper = pulled[ncoarse + 2 * blocks :]
        whole = lax.psum(coarse_part, ("grp", "tile"))
        own_share = lax.dynamic_slice_in_dim(whole, device * COARSE_DEV, COARSE_DEV, 0)
        from_above = shifted(lower, "tile", -1)
        from_below = shifted(upper, "tile", 1)
        pulled_here = middle + from_above + from_below
        pulled_here = pulled_here.at[:COARSE_DEV].add(own_share)
        return own_term + (latent_now - observed) / nugget - pulled_here

    start_grad = gradient(latent)
    half_momentum = momentum - 0.5 * leap_step * start_grad
    moved = latent + leap_step * half_momentum
    end_grad = gradient(moved)
    new_momentum = half_momentum - 0.5 * leap_step * end_grad
    return (moved, new_momentum)


def solution(mesh):
    in_specs = (
        P(("grp", "tile"), None),
        P(("grp", "tile"), None),
        P(("grp", "tile"), None),
        P(("grp", "tile"), None),
        P(("grp", "tile"), None, None),
        P(("grp", "tile"), None, None),
        P(),
        P(("grp", "tile"), None),
    )
    out_specs = (P(("grp", "tile"), None), P(("grp", "tile"), None))
    return jax.shard_map(
        on_device, mesh=mesh, in_specs=in_specs, out_specs=out_specs, check_vma=False
    )
```

profile of v0, /device:TPU:0, one launch (start us, length us, event | category | flops | bytes accessed | tf_op | source)
XLA Modules:
  0.0 196.9 jit_solution(14262933186287771185)
XLA Ops:
  0.6 0.0 copy-start
  0.6 0.0 copy-start.1
  0.7 1.4 collective-permute-start.1
  2.1 3.0 %collective-permute-start = (f32[16,128]{1,0:T(8,128)}, f32[16,128]{1,0:T(8,128)S(1)}, u32[]{:S(2)}, u32[]{:S(2)}) collective-permute-start(f32[16,128]{1,0:T(8,128)} %param.12), channel_id=1, source_target_pairs={{0,1},{1,2},{2,3},{3,4},{4,5},{5,6},{6,7},{8,9},{9,10},{10,11},{11... | collective-permute-start | bytes 24584 | tf_op jit(solution)/shard_map/ppermute | solution.py:19
  5.1 0.7 slice_bitcast_fusion.1
  5.8 0.7 compare_select_fusion.1
  6.5 0.9 select_reduce_fusion
  7.4 0.7 compare_convert_fusion
  8.1 0.1 copy.52
  8.1 0.1 mul.80
  8.2 0.1 copy.46
  8.3 0.1 reshape.116
  8.4 0.0 copy-done.1
  8.4 0.0 copy-start.8
  8.4 0.0 copy-start.3
  8.5 0.7 gather_fusion
  9.2 0.1 reshape.115
  9.3 0.1 copy.47
  9.3 0.0 copy-done.8
  9.4 0.1 copy.51
  9.5 0.1 reshape.124
  9.6 0.1 copy.53
  9.6 0.1 reshape.111
  9.7 43.3 %all-gather = f32[32,2,128]{2,1,0:T(2,128)S(1)} all-gather(f32[1,2,128]{2,1,0:T(2,128)S(1)} %slice_bitcast_fusion.1), channel_id=1, replica_groups=mesh['grp'=4,'tile'=8] {'grp','tile'}, dimensions={0}, use_global_device_ids=true | all-gather | bytes 33792 | tf_op jit(solution)/shard_map/all_gather | solution.py:51
  53.0 0.0 collective-permute-done.1
  53.0 0.0 collective-permute-done
  53.0 0.0 copy-done.3
  53.0 0.6 gather_fusion.1
  53.6 0.1 broadcast_multiply_fusion.1
  53.7 0.0 copy-done
  53.7 1.8 fusion.19
  55.5 0.0 copy-done.2
  55.5 0.0 copy-start.5
  55.6 0.0 copy-start.6
  55.6 0.0 copy-start.7
  55.6 1.7 convolution_bitcast_fusion.1
  57.3 1.0 fusion.20
  58.3 1.1 fusion.10
  59.4 0.8 scatter_custom_fusion
  60.2 1.3 collective-permute-start.2
  61.5 3.0 %collective-permute-start.3 = (f32[16,128]{1,0:T(8,128)S(1)}, f32[16,128]{1,0:T(8,128)S(1)}, u32[]{:S(2)}, u32[]{:S(2)}) collective-permute-start(f32[16,128]{1,0:T(8,128)S(1)} %get-tuple-element.31), channel_id=1, source_target_pairs={{0,1},{1,2},{2,3},{3,4},{4,5},{5,6},{6,7},{8,9},{9,10},{10,11},{11... | collective-permute-start | bytes 24584 | tf_op jit(solution)/shard_map/ppermute | solution.py:28
  64.6 37.1 %psum.14 = f32[64,128]{1,0:T(8,128)S(1)} all-reduce(f32[64,128]{1,0:T(8,128)S(1)} %slice.90), channel_id=1, replica_groups=mesh['grp'=4,'tile'=8] {'grp','tile'}, use_global_device_ids=true, to_apply=%region_2.3 | all-reduce | flops 8192 | bytes 65536 | tf_op jit(solution)/shard_map/psum | solution.py:72
  101.7 0.0 collective-permute-done.2
  101.7 0.0 collective-permute-done.3
  101.7 0.0 copy-done.5
  101.8 0.0 copy-start.4
  101.8 1.3 collective-permute-start.5
  103.1 3.0 %collective-permute-start.4 = (f32[16,128]{1,0:T(8,128)S(1)}, f32[16,128]{1,0:T(8,128)S(1)}, u32[]{:S(2)}, u32[]{:S(2)}) collective-permute-start(f32[16,128]{1,0:T(8,128)S(1)} %multiply_add_fusion), channel_id=1, source_target_pairs={{0,1},{1,2},{2,3},{3,4},{4,5},{5,6},{6,7},{8,9},{9,10},{10,11},{11... | collective-permute-start | bytes 24584 | tf_op jit(solution)/shard_map/ppermute | solution.py:19
  106.1 41.5 %all-gather.1 = f32[32,2,128]{2,1,0:T(2,128)S(1)} all-gather(f32[1,2,128]{2,1,0:T(2,128)S(1)} %slice_bitcast_fusion), channel_id=1, replica_groups=mesh['grp'=4,'tile'=8] {'grp','tile'}, dimensions={0}, use_global_device_ids=true | all-gather | bytes 33792 | tf_op jit(solution)/shard_map/all_gather | solution.py:51
  147.6 0.0 collective-permute-done.5
  147.6 0.0 collective-permute-done.4
  147.6 0.6 gather_fusion.2
  148.2 0.1 broadcast_multiply_fusion
  148.3 1.8 fusion.21
  150.1 1.7 convolution_bitcast_fusion
  151.9 1.0 fusion.22
  152.8 1.1 fusion.8
  154.0 0.8 scatter_custom_fusion.1
  154.8 1.3 collective-permute-start.6
  156.1 3.0 %collective-permute-start.7 = (f32[16,128]{1,0:T(8,128)S(1)}, f32[16,128]{1,0:T(8,128)S(1)}, u32[]{:S(2)}, u32[]{:S(2)}) collective-permute-start(f32[16,128]{1,0:T(8,128)S(1)} %get-tuple-element.29), channel_id=1, source_target_pairs={{0,1},{1,2},{2,3},{3,4},{4,5},{5,6},{6,7},{8,9},{9,10},{10,11},{11... | collective-permute-start | bytes 24584 | tf_op jit(solution)/shard_map/ppermute | solution.py:28
  159.1 37.1 %psum.15 = f32[64,128]{1,0:T(8,128)S(1)} all-reduce(f32[64,128]{1,0:T(8,128)S(1)} %slice.96), channel_id=1, replica_groups=mesh['grp'=4,'tile'=8] {'grp','tile'}, use_global_device_ids=true, to_apply=%region_4.5 | all-reduce | flops 8192 | bytes 65536 | tf_op jit(solution)/shard_map/psum | solution.py:72
  196.2 0.0 collective-permute-done.6
  196.2 0.0 collective-permute-done.7
  196.3 0.6 multiply_subtract_fusion
  (27 shorter events, 0.2 us)
Async XLA Ops:
  0.6 53.1 %copy-start = (f32[16,128,256]{2,1,0:T(8,128)S(1)}, f32[16,128,256]{2,1,0:T(8,128)}, u32[]{:S(2)}) copy-start(f32[16,128,256]{2,1,0:T(8,128)} %param.16) | copy-start | bytes 6291460
  0.6 7.8 %copy-start.1 = (s32[512]{0:T(512)S(1)}, s32[512]{0:T(512)}, u32[]{:S(2)}) copy-start(s32[512]{0:T(512)} %param.18) | copy-start | bytes 6148
  0.7 52.4 %collective-permute-start.1 = (f32[16,128]{1,0:T(8,128)}, f32[16,128]{1,0:T(8,128)S(1)}, u32[]{:S(2)}, u32[]{:S(2)}) collective-permute-start(f32[16,128]{1,0:T(8,128)} %param.12), channel_id=1, source_target_pairs={{1,0},{2,1},{3,2},{4,3},{5,4},{6,5},{7,6},{9,8},{10,9},{11,10},{12... | collective-permute-start | bytes 24584 | tf_op jit(solution)/shard_map/ppermute | solution.py:20
  2.1 50.9 %collective-permute-start = (f32[16,128]{1,0:T(8,128)}, f32[16,128]{1,0:T(8,128)S(1)}, u32[]{:S(2)}, u32[]{:S(2)}) collective-permute-start(f32[16,128]{1,0:T(8,128)} %param.12), channel_id=1, source_target_pairs={{0,1},{1,2},{2,3},{3,4},{4,5},{5,6},{6,7},{8,9},{9,10},{10,11},{11... | collective-permute-start | bytes 24584 | tf_op jit(solution)/shard_map/ppermute | solution.py:19
  8.4 0.9 copy-start.8
  8.4 44.6 %copy-start.3 = (f32[16,128]{1,0:T(8,128)S(1)}, f32[16,128]{1,0:T(8,128)}, u32[]{:S(2)}) copy-start(f32[16,128]{1,0:T(8,128)} %param.12) | copy-start | bytes 24580
  9.2 46.4 %copy-start.2 = (f32[16,128,128]{2,1,0:T(8,128)S(1)}, f32[16,128,128]{2,1,0:T(8,128)}, u32[]{:S(2)}) copy-start(f32[16,128,128]{2,1,0:T(8,128)} %param.17) | copy-start | bytes 3145732
  55.5 46.2 %copy-start.5 = (f32[16,128]{1,0:T(8,128)S(1)}, f32[16,128]{1,0:T(8,128)}, u32[]{:S(2)}) copy-start(f32[16,128]{1,0:T(8,128)} %param.13) | copy-start | bytes 24580
  55.6 46.2 %copy-start.6 = (f32[16,128]{1,0:T(8,128)S(1)}, f32[16,128]{1,0:T(8,128)}, u32[]{:S(2)}) copy-start(f32[16,128]{1,0:T(8,128)} %param.15) | copy-start | bytes 24580
  55.6 46.2 %copy-start.7 = (f32[16,128]{1,0:T(8,128)S(1)}, f32[16,128]{1,0:T(8,128)}, u32[]{:S(2)}) copy-start(f32[16,128]{1,0:T(8,128)} %param.14) | copy-start | bytes 24580
  60.2 41.4 %collective-permute-start.2 = (f32[16,128]{1,0:T(8,128)S(1)}, f32[16,128]{1,0:T(8,128)S(1)}, u32[]{:S(2)}, u32[]{:S(2)}) collective-permute-start(f32[16,128]{1,0:T(8,128)S(1)} %get-tuple-element.30), channel_id=1, source_target_pairs={{1,0},{2,1},{3,2},{4,3},{5,4},{6,5},{7,6},{9,8},{10,9},{11,10},{12... | collective-permute-start | bytes 24584 | tf_op jit(solution)/shard_map/ppermute | solution.py:28
  61.5 40.1 %collective-permute-start.3 = (f32[16,128]{1,0:T(8,128)S(1)}, f32[16,128]{1,0:T(8,128)S(1)}, u32[]{:S(2)}, u32[]{:S(2)}) collective-permute-start(f32[16,128]{1,0:T(8,128)S(1)} %get-tuple-element.31), channel_id=1, source_target_pairs={{0,1},{1,2},{2,3},{3,4},{4,5},{5,6},{6,7},{8,9},{9,10},{10,11},{11... | collective-permute-start | bytes 24584 | tf_op jit(solution)/shard_map/ppermute | solution.py:28
  101.8 94.5 %copy-start.4 = (f32[16,128]{1,0:T(8,128)}, f32[16,128]{1,0:T(8,128)S(1)}, u32[]{:S(2)}) copy-start(f32[16,128]{1,0:T(8,128)S(1)} %multiply_add_fusion) | copy-start | bytes 24580
  101.8 45.8 %collective-permute-start.5 = (f32[16,128]{1,0:T(8,128)S(1)}, f32[16,128]{1,0:T(8,128)S(1)}, u32[]{:S(2)}, u32[]{:S(2)}) collective-permute-start(f32[16,128]{1,0:T(8,128)S(1)} %multiply_add_fusion), channel_id=1, source_target_pairs={{1,0},{2,1},{3,2},{4,3},{5,4},{6,5},{7,6},{9,8},{10,9},{11,10},{12... | collective-permute-start | bytes 24584 | tf_op jit(solution)/shard_map/ppermute | solution.py:20
  103.1 44.5 %collective-permute-start.4 = (f32[16,128]{1,0:T(8,128)S(1)}, f32[16,128]{1,0:T(8,128)S(1)}, u32[]{:S(2)}, u32[]{:S(2)}) collective-permute-start(f32[16,128]{1,0:T(8,128)S(1)} %multiply_add_fusion), channel_id=1, source_target_pairs={{0,1},{1,2},{2,3},{3,4},{4,5},{5,6},{6,7},{8,9},{9,10},{10,11},{11... | collective-permute-start | bytes 24584 | tf_op jit(solution)/shard_map/ppermute | solution.py:19
  154.8 41.4 %collective-permute-start.6 = (f32[16,128]{1,0:T(8,128)S(1)}, f32[16,128]{1,0:T(8,128)S(1)}, u32[]{:S(2)}, u32[]{:S(2)}) collective-permute-start(f32[16,128]{1,0:T(8,128)S(1)} %get-tuple-element.28), channel_id=1, source_target_pairs={{1,0},{2,1},{3,2},{4,3},{5,4},{6,5},{7,6},{9,8},{10,9},{11,10},{12... | collective-permute-start | bytes 24584 | tf_op jit(solution)/shard_map/ppermute | solution.py:28
  156.1 40.1 %collective-permute-start.7 = (f32[16,128]{1,0:T(8,128)S(1)}, f32[16,128]{1,0:T(8,128)S(1)}, u32[]{:S(2)}, u32[]{:S(2)}) collective-permute-start(f32[16,128]{1,0:T(8,128)S(1)} %get-tuple-element.29), channel_id=1, source_target_pairs={{0,1},{1,2},{2,3},{3,4},{4,5},{5,6},{6,7},{8,9},{9,10},{10,11},{11... | collective-permute-start | bytes 24584 | tf_op jit(solution)/shard_map/ppermute | solution.py:28
where the time goes:
time: 198 us; the launch traced here: 197 us
  blocking collectives  159 us (80%)
  starting transfers between devices  17.4 us (9%)
  matrix products  11.3 us (6%)
  other arithmetic  4.7 us (2%)
  local copies, waits for them, and re-layouts  3.5 us (2%)
    all_gather x2, blocking collectives, gradient(): lax.all_gather(latent_now[:COARSE_DEV], ('grp', 'tile'), axis=0, tiled=True)  84.7 us
    psum x2, blocking collectives, gradient(): whole = lax.psum(coarse_part, ('grp', 'tile'))  74.2 us
    ppermute x4, starting transfers between devices, shifted(): lax.ppermute(value, axis, [(source, source + steps) for source in range(l...  8.65 us
    ppermute x2, starting transfers between devices, with_halo(): before = lax.ppermute(last, axis, up)  6.07 us
  transfers between devices with their start and end apart: 8, of which 0 were waited for; matrix products, arithmetic and copies ran while one was open for 2% of the time, Pallas kernels for 0%

commit v1 on v0

v1 whole, which is shorter than its diff:
```python
import functools

import jax
import jax.numpy as jnp
from jax import lax
from jax.experimental import pallas as pl
from jax.experimental.pallas import tpu as pltpu
from jax.sharding import PartitionSpec as P

COARSE_DEV = 2
ROWS = 8

leap_step = 0.25

MESH = pl.DeviceIdType.MESH
HIGHEST = lax.Precision.HIGHEST


def kernel(
    ngrp,
    ntile,
    latent_ref,
    momentum_ref,
    observed_ref,
    nugget_ref,
    cond_hbm,
    whiten_hbm,
    slot_ref,
    neigh_ref,
    moved_ref,
    newmom_ref,
    cond,
    whit,
    both,
    table,
    sent,
    landed,
    near,
    push,
    own,
    index,
    load_sem,
    send_sem,
    recv_sem,
    near_sem,
):
    blocks, width = latent_ref.shape
    devices = ngrp * ntile
    grp = lax.axis_index("grp")
    tile = lax.axis_index("tile")
    me = grp * ntile + tile
    halo = devices * ROWS
    absent = halo + 3 * blocks
    above = (grp, lax.rem(tile + 1, ntile))
    below = (grp, lax.rem(tile + ntile - 1, ntile))

    def peer(step):
        flat = lax.rem(me + step, devices)
        return flat, (flat // ntile, lax.rem(flat, ntile))

    loads = []
    pieces = load_sem.shape[1]
    part = blocks // pieces
    for i in range(pieces):
        rows = pl.ds(i * part, part)
        loads.append(
            (
                pltpu.make_async_copy(whiten_hbm.at[rows], whit.at[rows], load_sem.at[0, i]),
                pltpu.make_async_copy(cond_hbm.at[rows], cond.at[rows], load_sem.at[1, i]),
            )
        )
    for pair in loads:
        for copy in pair:
            copy.start()

    barrier = pltpu.get_barrier_semaphore()

    def greet(step, carry):
        pl.semaphore_signal(barrier, inc=1, device_id=peer(step)[1], device_id_type=MESH)
        return carry

    lax.fori_loop(1, devices, greet, 0)

    lanes = lax.broadcasted_iota(jnp.int32, (1, 6 * blocks), 1) % (2 * blocks)
    places = jnp.full((1, 6 * blocks), -1, jnp.int32)
    for s in range(blocks):
        for k in range(2):
            rank = neigh_ref[s, k]
            slot = slot_ref[rank]
            owner = slot // blocks
            place = lax.rem(slot, blocks)
            row = jnp.where(
                rank < COARSE_DEV * devices,
                owner * ROWS + place,
                halo + (owner - me + 1) * blocks + place,
            )
            row = jnp.where(slot == me * blocks + s, absent, row)
            index[k * blocks + s] = row
            places = jnp.where(lanes == k * blocks + s, row, places)
    hot = (lax.broadcasted_iota(jnp.int32, (absent, 6 * blocks), 0) == places)
    hot = hot.astype(jnp.float32).astype(jnp.bfloat16)
    for turn in range(2):
        table[turn, absent : absent + ROWS] = jnp.zeros((ROWS, width), jnp.float32)

    pl.semaphore_wait(barrier, devices - 1)

    def spread(turn, values):
        sends = []
        for side, (to, row) in enumerate(((above, halo), (below, halo + 2 * blocks))):
            copy = pltpu.make_async_remote_copy(
                src_ref=values,
                dst_ref=table.at[turn, pl.ds(row, blocks)],
                send_sem=near_sem.at[turn, 0, side],
                recv_sem=near_sem.at[turn, 1, side],
                device_id=to,
                device_id_type=MESH,
            )
            copy.start()
            sends.append(copy)

        def send(step, carry):
            pltpu.make_async_remote_copy(
                src_ref=values.at[pl.ds(0, COARSE_DEV)],
                dst_ref=table.at[turn, pl.ds(pl.multiple_of(me * ROWS, ROWS), COARSE_DEV)],
                send_sem=send_sem.at[turn],
                recv_sem=recv_sem.at[turn],
                device_id=peer(step)[1],
                device_id_type=MESH,
            ).start()
            return carry

        lax.fori_loop(1, devices, send, 0)
        table[turn, pl.ds(pl.multiple_of(me * ROWS, ROWS), COARSE_DEV)] = values[:COARSE_DEV]
        table[turn, halo + blocks : halo + 2 * blocks] = values[...]
        return sends

    def give(turn):
        sends = []
        for side, (to, row) in enumerate(((above, halo + 2 * blocks), (below, halo))):
            copy = pltpu.make_async_remote_copy(
                src_ref=sent.at[turn - 2, pl.ds(row, blocks)],
                dst_ref=near.at[turn - 2, side],
                send_sem=near_sem.at[turn, 0, side],
                recv_sem=near_sem.at[turn, 1, side],
                device_id=to,
                device_id_type=MESH,
            )
            copy.start()
            sends.append(copy)

        def send(step, carry):
            flat, to = peer(step)
            pltpu.make_async_remote_copy(
                src_ref=sent.at[turn - 2, pl.ds(pl.multiple_of(flat * ROWS, ROWS), COARSE_DEV)],
                dst_ref=landed.at[turn - 2, pl.ds(pl.multiple_of(me * ROWS, ROWS), COARSE_DEV)],
                send_sem=send_sem.at[turn],
                recv_sem=recv_sem.at[turn],
                device_id=to,
                device_id_type=MESH,
            ).start()
            return carry

        lax.fori_loop(1, devices, send, 0)
        mine = pl.ds(pl.multiple_of(me * ROWS, ROWS), ROWS)
        landed[turn - 2, mine] = sent[turn - 2, mine]
        return sends

    def arrive(turn, buffer, sends):
        for copy in sends:
            copy.wait_recv()
        amount = buffer.at[pl.ds(0, (devices - 1) * COARSE_DEV)]
        pltpu.make_async_copy(amount, amount, recv_sem.at[turn]).wait()

    def drain(turn, buffer, sends):
        for copy in sends:
            copy.wait_send()
        amount = buffer.at[pl.ds(0, (devices - 1) * COARSE_DEV)]
        pltpu.make_async_copy(amount, amount, send_sem.at[turn]).wait()

    first = spread(0, latent_ref)

    for i, pair in enumerate(loads):
        for copy in pair:
            copy.wait()
        for b in range(i * part, (i + 1) * part):
            square = lax.dot_general(
                whit[b], whit[b], (((0,), (0,)), ((), ())),
                precision=HIGHEST, preferred_element_type=jnp.float32,
            )
            both[b, :, :width] = square
            both[b, :, width:] = jnp.dot(
                square, cond[b], precision=HIGHEST, preferred_element_type=jnp.float32
            )

    diagonal = lax.broadcasted_iota(jnp.int32, (width, width), 0) == lax.broadcasted_iota(
        jnp.int32, (width, width), 1
    )

    def pushes(turn, values):
        for b in range(blocks):
            c0 = table[turn, pl.ds(index[b], 1), :]
            c1 = table[turn, pl.ds(index[blocks + b], 1), :]
            spreadout = jnp.where(diagonal, values[b : b + 1, :], 0.0)
            spreadout -= cond[b, :, :width] * c0 + cond[b, :, width:] * c1
            rest = jnp.sum(spreadout, axis=1, keepdims=True)
            out = jnp.sum(both[b] * rest, axis=0, keepdims=True)
            own[b : b + 1, :] = out[:, :width]
            push[b : b + 1, :] = out[:, width : 2 * width]
            push[blocks + b : blocks + b + 1, :] = out[:, 2 * width :]
        rest = push[...]
        split = []
        for _ in range(3):
            piece = rest.astype(jnp.bfloat16)
            split.append(piece)
            rest = rest - piece.astype(jnp.float32)
        sent[turn] = jnp.dot(
            hot, jnp.concatenate(split, axis=0), preferred_element_type=jnp.float32
        )

    def pulled(turn):
        total = landed[turn].reshape(devices, ROWS, width).sum(axis=0)
        row = lax.broadcasted_iota(jnp.int32, (ROWS, width), 0)
        total = jnp.where(row < COARSE_DEV, total, 0.0)
        total = jnp.concatenate(
            [total, jnp.zeros((blocks - ROWS, width), jnp.float32)], axis=0
        )
        return total + sent[turn, halo + blocks : halo + 2 * blocks] + near[turn, 0] + near[turn, 1]

    latent = latent_ref[...]
    arrive(0, table.at[0], first)
    pushes(0, latent_ref)
    second = give(2)
    known = own[...] + (latent - observed_ref[...]) / nugget_ref[...]
    arrive(2, landed.at[0], second)
    half = momentum_ref[...] - 0.5 * leap_step * (known - pulled(0))
    moved = latent + leap_step * half
    moved_ref[...] = moved
    third = spread(1, moved_ref)
    arrive(1, table.at[1], third)
    pushes(1, moved_ref)
    fourth = give(3)
    known = own[...] + (moved - observed_ref[...]) / nugget_ref[...]
    arrive(3, landed.at[1], fourth)
    newmom_ref[...] = half - 0.5 * leap_step * (known - pulled(1))
    drain(0, table.at[0], first)
    drain(2, landed.at[0], second)
    drain(1, table.at[1], third)
    drain(3, landed.at[1], fourth)


def on_device(latent, momentum, observed, nugget, cond_weights, whiten, slot_of_rank, neighbours):
    ngrp, ntile = lax.axis_size("grp"), lax.axis_size("tile")
    blocks, width = latent.shape
    devices = ngrp * ntile
    rows = devices * ROWS + 3 * blocks
    f32 = jnp.float32
    vmem = pl.BlockSpec(memory_space=pltpu.VMEM)
    smem = pl.BlockSpec(memory_space=pltpu.SMEM)
    anywhere = pl.BlockSpec(memory_space=pl.ANY)
    return pl.pallas_call(
        functools.partial(kernel, ngrp, ntile),
        out_shape=[jax.ShapeDtypeStruct((blocks, width), f32)] * 2,
        in_specs=[vmem] * 4 + [anywhere] * 2 + [smem] * 2,
        out_specs=[vmem] * 2,
        scratch_shapes=[
            pltpu.VMEM(cond_weights.shape, f32),
            pltpu.VMEM(whiten.shape, f32),
            pltpu.VMEM((blocks, width, 3 * width), f32),
            pltpu.VMEM((2, rows + ROWS, width), f32),
            pltpu.VMEM((2, rows, width), f32),
            pltpu.VMEM((2, devices * ROWS, width), f32),
            pltpu.VMEM((2, 2, blocks, width), f32),
            pltpu.VMEM((2 * blocks, width), f32),
            pltpu.VMEM((blocks, width), f32),
            pltpu.SMEM((2 * blocks,), jnp.int32),
            pltpu.SemaphoreType.DMA((2, 4)),
            pltpu.SemaphoreType.DMA((4,)),
            pltpu.SemaphoreType.DMA((4,)),
            pltpu.SemaphoreType.DMA((4, 2, 2)),
        ],
        compiler_params=pltpu.CompilerParams(
            collective_id=0, has_side_effects=True, vmem_limit_bytes=40 * 1024 * 1024
        ),
    )(latent, momentum, observed, nugget, cond_weights, whiten, slot_of_rank, neighbours)


def solution(mesh):
    split = P(("grp", "tile"), None)
    cube = P(("grp", "tile"), None, None)
    return jax.shard_map(
        on_device,
        mesh=mesh,
        in_specs=(split, split, split, split, cube, cube, P(), split),
        out_specs=(split, split),
        check_vma=False,
    )
```

time: 198 us -> 37.5 us (0.19)
  blocking collectives: 159 us -> 0 us
  Pallas kernels: 0 us -> 28.1 us
  starting transfers between devices: 17.4 us -> 0 us
  matrix products: 11.3 us -> 0 us
  local copies, waits for them, and re-layouts: 3.5 us -> 8.24 us
  other arithmetic: 4.7 us -> 0 us
    all_gather x2 -> x0, blocking collectives: 84.7 us -> none  [gradient(): lax.all_gather(latent_now[:COARSE_DEV], ('grp', 'tile'), axis=0, tiled=True)]
    psum x2 -> x0, blocking collectives: 74.2 us -> none  [gradient(): whole = lax.psum(coarse_part, ('grp', 'tile'))]
    pallas_call x0 -> x1, Pallas kernels: none -> 28.1 us  [on_device(): pl.pallas_call(functools.partial(kernel, ngrp, ntile), out_shape=[jax.Sha...]
    ppermute x8 -> x0, starting transfers between devices: 17.4 us -> none  [the longest x4 8.65 us: shifted(): lax.ppermute(value, axis, [(source, source + steps) for source in range(l...]
    dot_general x8 -> x0, matrix products: 11.3 us -> none  [the longest x2 3.65 us: gradient(): jnp.einsum('bij,bj->bi', cond_weights, cond_values, precision=lax.Precisi...]
    unnamed x20 -> x17, local copies, waits for them, and re-layouts: 0.76 us -> 8.24 us
    gather x5 -> x0, local copies, waits for them, and re-layouts: 2.02 us -> none  [the longest x2 1.15 us: gradient(): lookup[lookup_index] * present[:, :, None]]
  transfers between devices with their start and end apart: 8 -> 0, of which waited for: 0 -> 0; matrix products, arithmetic and copies ran while one was open for 2% -> 0% of each run, Pallas kernels for 0% -> 0%
where the time goes in v1:
time: 37.5 us; the launch traced here: 37 us
  Pallas kernels  28.1 us (75%)
  local copies, waits for them, and re-layouts  8.24 us (22%)
  between operations  0.65 us (2%)
    pallas_call x1, Pallas kernels, on_device(): pl.pallas_call(functools.partial(kernel, ngrp, ntile), out_shape=[jax.Sha...  28.1 us
    unnamed x17, local copies, waits for them, and re-layouts  8.24 us

profile of v1, /device:TPU:0, one launch (start us, length us, event | category | flops | bytes accessed | tf_op | source)
XLA Modules:
  0.0 37.0 jit_solution(2021240157233240335)
XLA Ops:
  0.6 0.8 %copy.10.neigh_ref = s32[16,2]{1,0:T(8,128)S(1)} copy(s32[16,2]{0,1:T(2,128)} %param.15) | data formatting | bytes 256 | tf_op args[7]
  1.4 0.0 copy-start
  1.4 1.6 %copy-done = f32[16,128,256]{2,1,0:T(8,128)S(1)} copy-done((f32[16,128,256]{2,1,0:T(8,128)S(1)}, f32[16,128,256]{2,1,0:T(8,128)}, u32[]{:S(2)}) %copy-start) | copy-done | bytes 2097176
  3.0 0.0 copy-start.1
  3.0 1.2 %copy-done.1 = f32[16,128,128]{2,1,0:T(8,128)S(1)} copy-done((f32[16,128,128]{2,1,0:T(8,128)S(1)}, f32[16,128,128]{2,1,0:T(8,128)}, u32[]{:S(2)}) %copy-start.1) | copy-done | bytes 1048600
  4.2 0.0 copy-start.2
  4.2 0.7 %copy-done.2 = f32[16,128]{1,0:T(8,128)S(1)} copy-done((f32[16,128]{1,0:T(8,128)S(1)}, f32[16,128]{1,0:T(8,128)}, u32[]{:S(2)}) %copy-start.2) | copy-done | bytes 8216
  4.9 0.0 copy-start.3
  4.9 0.7 %copy-done.3 = f32[16,128]{1,0:T(8,128)S(1)} copy-done((f32[16,128]{1,0:T(8,128)S(1)}, f32[16,128]{1,0:T(8,128)}, u32[]{:S(2)}) %copy-start.3) | copy-done | bytes 8216
  5.6 0.0 copy-start.4
  5.6 0.7 %copy-done.4 = f32[16,128]{1,0:T(8,128)S(1)} copy-done((f32[16,128]{1,0:T(8,128)S(1)}, f32[16,128]{1,0:T(8,128)}, u32[]{:S(2)}) %copy-start.4) | copy-done | bytes 8216
  6.3 0.0 copy-start.5
  6.3 0.7 %copy-done.5 = f32[16,128]{1,0:T(8,128)S(1)} copy-done((f32[16,128]{1,0:T(8,128)S(1)}, f32[16,128]{1,0:T(8,128)}, u32[]{:S(2)}) %copy-start.5) | copy-done | bytes 8216
  7.0 0.0 copy-start.6
  7.0 0.7 %copy-done.6 = s32[512]{0:T(512)S(1)} copy-done((s32[512]{0:T(512)S(1)}, s32[512]{0:T(512)}, u32[]{:S(2)}) %copy-start.6) | copy-done | bytes 2072
  7.7 28.1 %shard_map.95 = (f32[16,128]{1,0:T(8,128)S(1)}, f32[16,128]{1,0:T(8,128)S(1)}) custom-call(f32[16,128]{1,0:T(8,128)S(1)} %copy-done.2, f32[16,128]{1,0:T(8,128)S(1)} %copy-done.3, f32[16,128]{1,0:T(8,128)S(1)} %copy-done.4, f32[16,128]{1,0:T(8,128)S(1)} %copy-done.5, f32[16,128,256]{2,1,0:T(8,128)S(1)} %copy-done, f32[16,128,128]{2,1,0:T(8,128)S(1)} %copy-done.1, ...), custom_call_target="tpu_custom_call" | custom-call | tf_op jit(solution)/shard_map/pallas_call | solution.py:260
  35.8 0.6 %copy.13 = f32[16,128]{1,0:T(8,128)} copy(f32[16,128]{1,0:T(8,128)S(1)} %get-tuple-element.4) | data formatting | bytes 16384
  36.4 0.6 %copy.14 = f32[16,128]{1,0:T(8,128)} copy(f32[16,128]{1,0:T(8,128)S(1)} %get-tuple-element.5) | data formatting | bytes 16384
Async XLA Ops:
  1.4 1.6 %copy-start = (f32[16,128,256]{2,1,0:T(8,128)S(1)}, f32[16,128,256]{2,1,0:T(8,128)}, u32[]{:S(2)}) copy-start(f32[16,128,256]{2,1,0:T(8,128)} %cond_hbm.1) | copy-start | bytes 6291460
  3.0 1.2 %copy-start.1 = (f32[16,128,128]{2,1,0:T(8,128)S(1)}, f32[16,128,128]{2,1,0:T(8,128)}, u32[]{:S(2)}) copy-start(f32[16,128,128]{2,1,0:T(8,128)} %whiten_hbm.1) | copy-start | bytes 3145732
  4.2 0.7 %copy-start.2 = (f32[16,128]{1,0:T(8,128)S(1)}, f32[16,128]{1,0:T(8,128)}, u32[]{:S(2)}) copy-start(f32[16,128]{1,0:T(8,128)} %latent_ref.1) | copy-start | bytes 24580
  4.9 0.7 %copy-start.3 = (f32[16,128]{1,0:T(8,128)S(1)}, f32[16,128]{1,0:T(8,128)}, u32[]{:S(2)}) copy-start(f32[16,128]{1,0:T(8,128)} %momentum_ref.1) | copy-start | bytes 24580
  5.6 0.7 %copy-start.4 = (f32[16,128]{1,0:T(8,128)S(1)}, f32[16,128]{1,0:T(8,128)}, u32[]{:S(2)}) copy-start(f32[16,128]{1,0:T(8,128)} %observed_ref.1) | copy-start | bytes 24580
  6.3 0.7 %copy-start.5 = (f32[16,128]{1,0:T(8,128)S(1)}, f32[16,128]{1,0:T(8,128)}, u32[]{:S(2)}) copy-start(f32[16,128]{1,0:T(8,128)} %nugget_ref.1) | copy-start | bytes 24580
  7.0 0.7 %copy-start.6 = (s32[512]{0:T(512)S(1)}, s32[512]{0:T(512)}, u32[]{:S(2)}) copy-start(s32[512]{0:T(512)} %slot_ref.1) | copy-start | bytes 6148

commit v2 on v1

--- a/solution.py
+++ b/solution.py
@@ -13,22 +13,32 @@
 leap_step = 0.25
 
 MESH = pl.DeviceIdType.MESH
-HIGHEST = lax.Precision.HIGHEST
+
+
+def halves(x):
+    high = x.astype(jnp.bfloat16)
+    return high, (x - high.astype(jnp.float32)).astype(jnp.bfloat16)
 
 
 def kernel(
     ngrp,
     ntile,
+    latent_hbm,
+    momentum_hbm,
+    observed_hbm,
+    nugget_hbm,
+    cond_hbm,
+    whiten_hbm,
+    slot_hbm,
+    neigh_hbm,
+    moved_ref,
+    newmom_ref,
     latent_ref,
     momentum_ref,
     observed_ref,
     nugget_ref,
-    cond_hbm,
-    whiten_hbm,
     slot_ref,
     neigh_ref,
-    moved_ref,
-    newmom_ref,
     cond,
     whit,
     both,
@@ -39,6 +49,7 @@
     push,
     own,
     index,
+    small_sem,
     load_sem,
     send_sem,
     recv_sem,
@@ -58,6 +69,21 @@
         flat = lax.rem(me + step, devices)
         return flat, (flat // ntile, lax.rem(flat, ntile))
 
+    small = [
+        pltpu.make_async_copy(source, target, small_sem.at[i])
+        for i, (source, target) in enumerate(
+            (
+                (neigh_hbm, neigh_ref),
+                (slot_hbm, slot_ref),
+                (latent_hbm, latent_ref),
+                (momentum_hbm, momentum_ref),
+                (observed_hbm, observed_ref),
+                (nugget_hbm, nugget_ref),
+            )
+        )
+    ]
+    for copy in small:
+        copy.start()
     loads = []
     pieces = load_sem.shape[1]
     part = blocks // pieces
@@ -81,11 +107,14 @@
 
     lax.fori_loop(1, devices, greet, 0)
 
+    small[0].wait()
+    small[1].wait()
+
     lanes = lax.broadcasted_iota(jnp.int32, (1, 6 * blocks), 1) % (2 * blocks)
     places = jnp.full((1, 6 * blocks), -1, jnp.int32)
     for s in range(blocks):
         for k in range(2):
-            rank = neigh_ref[s, k]
+            rank = neigh_ref[k, s]
             slot = slot_ref[rank]
             owner = slot // blocks
             place = lax.rem(slot, blocks)
@@ -102,6 +131,8 @@
     for turn in range(2):
         table[turn, absent : absent + ROWS] = jnp.zeros((ROWS, width), jnp.float32)
 
+    for copy in small[2:]:
+        copy.wait()
     pl.semaphore_wait(barrier, devices - 1)
 
     def spread(turn, values):
@@ -183,13 +214,20 @@
         for copy in pair:
             copy.wait()
         for b in range(i * part, (i + 1) * part):
+            high, low = halves(whit[b])
             square = lax.dot_general(
-                whit[b], whit[b], (((0,), (0,)), ((), ())),
-                precision=HIGHEST, preferred_element_type=jnp.float32,
+                jnp.concatenate([high, high, low], axis=0),
+                jnp.concatenate([high, low, high], axis=0),
+                (((0,), (0,)), ((), ())),
+                preferred_element_type=jnp.float32,
             )
             both[b, :, :width] = square
+            left_high, left_low = halves(square)
+            high, low = halves(cond[b])
             both[b, :, width:] = jnp.dot(
-                square, cond[b], precision=HIGHEST, preferred_element_type=jnp.float32
+                jnp.concatenate([left_high, left_high, left_low], axis=1),
+                jnp.concatenate([high, low, high], axis=0),
+                preferred_element_type=jnp.float32,
             )
 
     diagonal = lax.broadcasted_iota(jnp.int32, (width, width), 0) == lax.broadcasted_iota(
@@ -255,14 +293,16 @@
     rows = devices * ROWS + 3 * blocks
     f32 = jnp.float32
     vmem = pl.BlockSpec(memory_space=pltpu.VMEM)
-    smem = pl.BlockSpec(memory_space=pltpu.SMEM)
-    anywhere = pl.BlockSpec(memory_space=pl.ANY)
+    anywhere = pl.BlockSpec(memory_space=pltpu.HBM)
     return pl.pallas_call(
         functools.partial(kernel, ngrp, ntile),
         out_shape=[jax.ShapeDtypeStruct((blocks, width), f32)] * 2,
-        in_specs=[vmem] * 4 + [anywhere] * 2 + [smem] * 2,
+        in_specs=[anywhere] * 8,
         out_specs=[vmem] * 2,
         scratch_shapes=[
+            *[pltpu.VMEM((blocks, width), f32)] * 4,
+            pltpu.SMEM(slot_of_rank.shape, jnp.int32),
+            pltpu.SMEM((2, blocks), jnp.int32),
             pltpu.VMEM(cond_weights.shape, f32),
             pltpu.VMEM(whiten.shape, f32),
             pltpu.VMEM((blocks, width, 3 * width), f32),
@@ -273,15 +313,16 @@
             pltpu.VMEM((2 * blocks, width), f32),
             pltpu.VMEM((blocks, width), f32),
             pltpu.SMEM((2 * blocks,), jnp.int32),
+            pltpu.SemaphoreType.DMA((6,)),
             pltpu.SemaphoreType.DMA((2, 4)),
             pltpu.SemaphoreType.DMA((4,)),
             pltpu.SemaphoreType.DMA((4,)),
             pltpu.SemaphoreType.DMA((4, 2, 2)),
         ],
         compiler_params=pltpu.CompilerParams(
-            collective_id=0, has_side_effects=True, vmem_limit_bytes=40 * 1024 * 1024
+            collective_id=0, has_side_effects=True, vmem_limit_bytes=60 * 1024 * 1024
         ),
-    )(latent, momentum, observed, nugget, cond_weights, whiten, slot_of_rank, neighbours)
+    )(latent, momentum, observed, nugget, cond_weights, whiten, slot_of_rank, neighbours.T)
 
 
 def solution(mesh):

time: 37.5 us -> 31.4 us (0.84)
  local copies, waits for them, and re-layouts: 8.24 us -> 2.59 us
    unnamed x17 -> x2, local copies, waits for them, and re-layouts: 8.24 us -> 2.59 us
where the time goes in v2:
time: 31.4 us; the launch traced here: 31.1 us
  Pallas kernels  27.9 us (89%)
  local copies, waits for them, and re-layouts  2.59 us (8%)
  between operations  0.64 us (2%)
    pallas_call x1, Pallas kernels, on_device(): pl.pallas_call(functools.partial(kernel, ngrp, ntile), out_shape=[jax.Sha...  27.9 us
    unnamed x2, local copies, waits for them, and re-layouts  2.59 us

profile of v2, /device:TPU:0, one launch (start us, length us, event | category | flops | bytes accessed | tf_op | source)
XLA Modules:
  0.0 31.1 jit_solution(12358142434492401896)
XLA Ops:
  0.6 27.9 %shard_map.95 = (f32[16,128]{1,0:T(8,128)}, f32[16,128]{1,0:T(8,128)}) custom-call(f32[16,128]{1,0:T(8,128)} %latent_hbm.1, f32[16,128]{1,0:T(8,128)} %momentum_hbm.1, f32[16,128]{1,0:T(8,128)} %observed_hbm.1, f32[16,128]{1,0:T(8,128)} %nugget_hbm.1, f32[16,128,256]{2,1,0:T(8,128)} %cond_hbm.1, f32[16,128,128]{2,1,0:T(8,128)} %whiten_hbm.1, s32[512]{0:T(512)} %slot_hbm.1, ...), custom_call_target="tpu_custom_call" | custom-call | tf_op jit(solution)/shard_map/pallas_call | solution.py:297
  28.5 1.3 %copy.12 = f32[16,128]{1,0:T(8,128)} copy(f32[16,128]{1,0:T(8,128)} %get-tuple-element.4) | data formatting | bytes 16384
  29.8 1.3 %copy.13 = f32[16,128]{1,0:T(8,128)} copy(f32[16,128]{1,0:T(8,128)} %get-tuple-element.5) | data formatting | bytes 16384

commit v3 on v2

--- a/solution.py
+++ b/solution.py
@@ -31,8 +31,8 @@
     whiten_hbm,
     slot_hbm,
     neigh_hbm,
-    moved_ref,
-    newmom_ref,
+    half_ref,
+    grad_ref,
     latent_ref,
     momentum_ref,
     observed_ref,
@@ -48,6 +48,8 @@
     near,
     push,
     own,
+    fine,
+    coarse,
     index,
     small_sem,
     load_sem,
@@ -65,9 +67,22 @@
     above = (grp, lax.rem(tile + 1, ntile))
     below = (grp, lax.rem(tile + ntile - 1, ntile))
 
-    def peer(step):
-        flat = lax.rem(me + step, devices)
-        return flat, (flat // ntile, lax.rem(flat, ntile))
+    def everyone(act):
+        if devices <= 64:
+            groups = [lax.rem(grp + a, ngrp) for a in range(ngrp)]
+            tiles = [lax.rem(tile + b, ntile) for b in range(ntile)]
+            for a in [*range(1, ngrp), 0]:
+                for b in reversed(range(ntile)):
+                    if a or b:
+                        act(groups[a] * ntile + tiles[b], (groups[a], tiles[b]))
+        else:
+
+            def body(step, carry):
+                flat = lax.rem(me + step, devices)
+                act(flat, (flat // ntile, lax.rem(flat, ntile)))
+                return carry
+
+            lax.fori_loop(1, devices, body, 0)
 
     small = [
         pltpu.make_async_copy(source, target, small_sem.at[i])
@@ -101,15 +116,92 @@
 
     barrier = pltpu.get_barrier_semaphore()
 
-    def greet(step, carry):
-        pl.semaphore_signal(barrier, inc=1, device_id=peer(step)[1], device_id_type=MESH)
-        return carry
-
-    lax.fori_loop(1, devices, greet, 0)
-
+    def greet(flat, to):
+        pl.semaphore_signal(barrier, inc=1, device_id=to, device_id_type=MESH)
+
+    everyone(greet)
+    pl.semaphore_wait(barrier, devices - 1)
+
+    my_rows = pl.ds(pl.multiple_of(me * ROWS, ROWS), COARSE_DEV)
+
+    def spread_coarse(turn, values):
+        def send(flat, to):
+            pltpu.make_async_remote_copy(
+                src_ref=values,
+                dst_ref=table.at[turn, my_rows],
+                send_sem=send_sem.at[turn],
+                recv_sem=recv_sem.at[turn],
+                device_id=to,
+                device_id_type=MESH,
+            ).start()
+
+        everyone(send)
+
+    def spread_near(turn, values):
+        sends = []
+        for side, (to, row) in enumerate(((above, halo), (below, halo + 2 * blocks))):
+            copy = pltpu.make_async_remote_copy(
+                src_ref=values,
+                dst_ref=table.at[turn, pl.ds(row, blocks)],
+                send_sem=near_sem.at[turn, 0, side],
+                recv_sem=near_sem.at[turn, 1, side],
+                device_id=to,
+                device_id_type=MESH,
+            )
+            copy.start()
+            sends.append(copy)
+        return sends
+
+    def give(turn):
+        def send(flat, to):
+            pltpu.make_async_remote_copy(
+                src_ref=sent.at[turn - 2, pl.ds(pl.multiple_of(flat * ROWS, ROWS), COARSE_DEV)],
+                dst_ref=landed.at[turn - 2, my_rows],
+                send_sem=send_sem.at[turn],
+                recv_sem=recv_sem.at[turn],
+                device_id=to,
+                device_id_type=MESH,
+            ).start()
+
+        everyone(send)
+        sends = []
+        for side, (to, row) in enumerate(((above, halo + 2 * blocks), (below, halo))):
+            copy = pltpu.make_async_remote_copy(
+                src_ref=sent.at[turn - 2, pl.ds(row, blocks)],
+                dst_ref=near.at[turn - 2, side],
+                send_sem=near_sem.at[turn, 0, side],
+                recv_sem=near_sem.at[turn, 1, side],
+                device_id=to,
+                device_id_type=MESH,
+            )
+            copy.start()
+            sends.append(copy)
+        mine = pl.ds(pl.multiple_of(me * ROWS, ROWS), ROWS)
+        landed[turn - 2, mine] = sent[turn - 2, mine]
+        return sends
+
+    def arrive_near(sends):
+        for copy in sends:
+            copy.wait_recv()
+
+    def arrive_coarse(turn, buffer):
+        amount = buffer.at[pl.ds(0, (devices - 1) * COARSE_DEV)]
+        pltpu.make_async_copy(amount, amount, recv_sem.at[turn]).wait()
+
+    def drain(turn, buffer, sends):
+        for copy in sends:
+            copy.wait_send()
+        amount = buffer.at[pl.ds(0, (devices - 1) * COARSE_DEV)]
+        pltpu.make_async_copy(amount, amount, send_sem.at[turn]).wait()
+
+    def keep(turn, values):
+        table[turn, my_rows] = values[:COARSE_DEV]
+        table[turn, halo + blocks : halo + 2 * blocks] = values
+
+    spread_coarse(0, latent_hbm.at[pl.ds(0, COARSE_DEV)])
+    first = spread_near(0, latent_hbm)
     small[0].wait()
     small[1].wait()
-
     lanes = lax.broadcasted_iota(jnp.int32, (1, 6 * blocks), 1) % (2 * blocks)
     places = jnp.full((1, 6 * blocks), -1, jnp.int32)
     for s in range(blocks):
@@ -133,82 +225,8 @@
 
     for copy in small[2:]:
         copy.wait()
-    pl.semaphore_wait(barrier, devices - 1)
-
-    def spread(turn, values):
-        sends = []
-        for side, (to, row) in enumerate(((above, halo), (below, halo + 2 * blocks))):
-            copy = pltpu.make_async_remote_copy(
-                src_ref=values,
-                dst_ref=table.at[turn, pl.ds(row, blocks)],
-                send_sem=near_sem.at[turn, 0, side],
-                recv_sem=near_sem.at[turn, 1, side],
-                device_id=to,
-                device_id_type=MESH,
-            )
-            copy.start()
-            sends.append(copy)
-
-        def send(step, carry):
-            pltpu.make_async_remote_copy(
-                src_ref=values.at[pl.ds(0, COARSE_DEV)],
-                dst_ref=table.at[turn, pl.ds(pl.multiple_of(me * ROWS, ROWS), COARSE_DEV)],
-                send_sem=send_sem.at[turn],
-                recv_sem=recv_sem.at[turn],
-                device_id=peer(step)[1],
-                device_id_type=MESH,
-            ).start()
-            return carry
-
-        lax.fori_loop(1, devices, send, 0)
-        table[turn, pl.ds(pl.multiple_of(me * ROWS, ROWS), COARSE_DEV)] = values[:COARSE_DEV]
-        table[turn, halo + blocks : halo + 2 * blocks] = values[...]
-        return sends
-
-    def give(turn):
-        sends = []
-        for side, (to, row) in enumerate(((above, halo + 2 * blocks), (below, halo))):
-            copy = pltpu.make_async_remote_copy(
-                src_ref=sent.at[turn - 2, pl.ds(row, blocks)],
-                dst_ref=near.at[turn - 2, side],
-                send_sem=near_sem.at[turn, 0, side],
-                recv_sem=near_sem.at[turn, 1, side],
-                device_id=to,
-                device_id_type=MESH,
-            )
-            copy.start()
-            sends.append(copy)
-
-        def send(step, carry):
-            flat, to = peer(step)
-            pltpu.make_async_remote_copy(
-                src_ref=sent.at[turn - 2, pl.ds(pl.multiple_of(flat * ROWS, ROWS), COARSE_DEV)],
-                dst_ref=landed.at[turn - 2, pl.ds(pl.multiple_of(me * ROWS, ROWS), COARSE_DEV)],
-                send_sem=send_sem.at[turn],
-                recv_sem=recv_sem.at[turn],
-                device_id=to,
-                device_id_type=MESH,
-            ).start()
-            return carry
-
-        lax.fori_loop(1, devices, send, 0)
-        mine = pl.ds(pl.multiple_of(me * ROWS, ROWS), ROWS)
-        landed[turn - 2, mine] = sent[turn - 2, mine]
-        return sends
-
-    def arrive(turn, buffer, sends):
-        for copy in sends:
-            copy.wait_recv()
-        amount = buffer.at[pl.ds(0, (devices - 1) * COARSE_DEV)]
-        pltpu.make_async_copy(amount, amount, recv_sem.at[turn]).wait()
-
-    def drain(turn, buffer, sends):
-        for copy in sends:
-            copy.wait_send()
-        amount = buffer.at[pl.ds(0, (devices - 1) * COARSE_DEV)]
-        pltpu.make_async_copy(amount, amount, send_sem.at[turn]).wait()
-
-    first = spread(0, latent_ref)
+    latent = latent_ref[...]
+    keep(0, latent)
 
     for i, pair in enumerate(loads):
         for copy in pair:
@@ -255,31 +273,42 @@
             hot, jnp.concatenate(split, axis=0), preferred_element_type=jnp.float32
         )
 
-    def pulled(turn):
+    def pulled_coarse(turn):
         total = landed[turn].reshape(devices, ROWS, width).sum(axis=0)
         row = lax.broadcasted_iota(jnp.int32, (ROWS, width), 0)
         total = jnp.where(row < COARSE_DEV, total, 0.0)
-        total = jnp.concatenate(
+        return jnp.concatenate(
             [total, jnp.zeros((blocks - ROWS, width), jnp.float32)], axis=0
         )
-        return total + sent[turn, halo + blocks : halo + 2 * blocks] + near[turn, 0] + near[turn, 1]
-
-    latent = latent_ref[...]
-    arrive(0, table.at[0], first)
-    pushes(0, latent_ref)
+
+    def pulled_near(turn):
+        return sent[turn, halo + blocks : halo + 2 * blocks] + near[turn, 0] + near[turn, 1]
+
+    arrive_near(first)
+    arrive_coarse(0, table.at[0])
+    pushes(0, latent)
     second = give(2)
     known = own[...] + (latent - observed_ref[...]) / nugget_ref[...]
-    arrive(2, landed.at[0], second)
-    half = momentum_ref[...] - 0.5 * leap_step * (known - pulled(0))
+    arrive_near(second)
+    half = momentum_ref[...] - 0.5 * leap_step * (known - pulled_near(0))
+    fine[...] = latent + leap_step * half
+    third = spread_near(1, fine)
+    arrive_coarse(2, landed.at[0])
+    half = half + 0.5 * leap_step * pulled_coarse(0)
     moved = latent + leap_step * half
-    moved_ref[...] = moved
-    third = spread(1, moved_ref)
-    arrive(1, table.at[1], third)
-    pushes(1, moved_ref)
+    coarse[...] = moved[:ROWS]
+    spread_coarse(1, coarse.at[pl.ds(0, COARSE_DEV)])
+    half_ref[...] = half
+    keep(1, moved)
+    arrive_near(third)
+    arrive_coarse(1, table.at[1])
+    pushes(1, moved)
     fourth = give(3)
     known = own[...] + (moved - observed_ref[...]) / nugget_ref[...]
-    arrive(3, landed.at[1], fourth)
-    newmom_ref[...] = half - 0.5 * leap_step * (known - pulled(1))
+    arrive_near(fourth)
+    known = known - pulled_near(1)
+    arrive_coarse(3, landed.at[1])
+    grad_ref[...] = known - pulled_coarse(1)
     drain(0, table.at[0], first)
     drain(2, landed.at[0], second)
     drain(1, table.at[1], third)
@@ -294,7 +323,7 @@
     f32 = jnp.float32
     vmem = pl.BlockSpec(memory_space=pltpu.VMEM)
     anywhere = pl.BlockSpec(memory_space=pltpu.HBM)
-    return pl.pallas_call(
+    half, end_grad = pl.pallas_call(
         functools.partial(kernel, ngrp, ntile),
         out_shape=[jax.ShapeDtypeStruct((blocks, width), f32)] * 2,
         in_specs=[anywhere] * 8,
@@ -312,6 +341,8 @@
             pltpu.VMEM((2, 2, blocks, width), f32),
             pltpu.VMEM((2 * blocks, width), f32),
             pltpu.VMEM((blocks, width), f32),
+            pltpu.VMEM((blocks, width), f32),
+            pltpu.VMEM((ROWS, width), f32),
             pltpu.SMEM((2 * blocks,), jnp.int32),
             pltpu.SemaphoreType.DMA((6,)),
             pltpu.SemaphoreType.DMA((2, 4)),
@@ -323,6 +354,7 @@
             collective_id=0, has_side_effects=True, vmem_limit_bytes=60 * 1024 * 1024
         ),
     )(latent, momentum, observed, nugget, cond_weights, whiten, slot_of_rank, neighbours.T)
+    return latent + leap_step * half, half - 0.5 * leap_step * end_grad
 
 
 def solution(mesh):

time: 31.4 us -> 30.3 us (0.965)
  local copies, waits for them, and re-layouts: 2.59 us -> 0.01 us
  other arithmetic: 0 us -> 1.32 us
    unnamed x2, local copies, waits for them, and re-layouts: 2.59 us -> 0.01 us
    sub x0 -> x1, other arithmetic: none -> 1.32 us  [on_device(): return (latent + leap_step * half, half - 0.5 * leap_step * end_grad)]
where the time goes in v3:
time: 30.3 us; the launch traced here: 30.1 us
  Pallas kernels  28.1 us (93%)
  other arithmetic  1.32 us (4%)
  between operations  0.66 us (2%)
    pallas_call x1, Pallas kernels, on_device(): pl.pallas_call(functools.partial(kernel, ngrp, ntile), out_shape=[jax.Sha...  28.1 us
    sub x1, other arithmetic, on_device(): return (latent + leap_step * half, half - 0.5 * leap_step * end_grad)  1.32 us

profile of v3, /device:TPU:0, one launch (start us, length us, event | category | flops | bytes accessed | tf_op | source)
XLA Modules:
  0.0 30.1 jit_solution(880018566761551722)
XLA Ops:
  0.6 0.0 copy-start
  0.6 28.1 %shard_map.95 = (f32[16,128]{1,0:T(8,128)}, f32[16,128]{1,0:T(8,128)}) custom-call(f32[16,128]{1,0:T(8,128)} %latent_hbm.1, f32[16,128]{1,0:T(8,128)} %momentum_hbm.1, f32[16,128]{1,0:T(8,128)} %observed_hbm.1, f32[16,128]{1,0:T(8,128)} %nugget_hbm.1, f32[16,128,256]{2,1,0:T(8,128)} %cond_hbm.1, f32[16,128,128]{2,1,0:T(8,128)} %whiten_hbm.1, s32[512]{0:T(512)} %slot_hbm.1, ...), custom_call_target="tpu_custom_call" | custom-call | tf_op jit(solution)/shard_map/pallas_call | solution.py:326
  28.7 0.0 copy-done
  28.7 1.3 %multiply_subtract_fusion = (f32[16,128]{1,0:T(8,128)}, f32[16,128]{1,0:T(8,128)}) fusion(f32[16,128]{1,0:T(8,128)} %get-tuple-element.4, f32[16,128]{1,0:T(8,128)} %get-tuple-element.5, f32[16,128]{1,0:T(8,128)S(1)} %copy-done), kind=kLoop, calls=%fused_computation | loop fusion | flops 8192 | bytes 40960 | tf_op jit(solution)/shard_map/sub | solution.py:357
Async XLA Ops:
  0.6 28.1 %copy-start = (f32[16,128]{1,0:T(8,128)S(1)}, f32[16,128]{1,0:T(8,128)}, u32[]{:S(2)}) copy-start(f32[16,128]{1,0:T(8,128)} %latent_hbm.1) | copy-start | bytes 24580

commit v4 on v3

--- a/solution.py
+++ b/solution.py
@@ -84,6 +84,13 @@
 
             lax.fori_loop(1, devices, body, 0)
 
+    barrier = pltpu.get_barrier_semaphore()
+
+    def greet(flat, to):
+        pl.semaphore_signal(barrier, inc=1, device_id=to, device_id_type=MESH)
+
+    everyone(greet)
+
     small = [
         pltpu.make_async_copy(source, target, small_sem.at[i])
         for i, (source, target) in enumerate(
@@ -114,12 +121,6 @@
         for copy in pair:
             copy.start()
 
-    barrier = pltpu.get_barrier_semaphore()
-
-    def greet(flat, to):
-        pl.semaphore_signal(barrier, inc=1, device_id=to, device_id_type=MESH)
-
-    everyone(greet)
     pl.semaphore_wait(barrier, devices - 1)
 
     my_rows = pl.ds(pl.multiple_of(me * ROWS, ROWS), COARSE_DEV)
@@ -325,7 +326,7 @@
     anywhere = pl.BlockSpec(memory_space=pltpu.HBM)
     half, end_grad = pl.pallas_call(
         functools.partial(kernel, ngrp, ntile),
-        out_shape=[jax.ShapeDtypeStruct((blocks, width), f32)] * 2,
+        out_shape=[pltpu.VMEM((blocks, width), f32)] * 2,
         in_specs=[anywhere] * 8,
         out_specs=[vmem] * 2,
         scratch_shapes=[

time: 30.3 us -> 28.9 us (0.954)
  other arithmetic: 1.32 us -> 0.61 us
  Pallas kernels: 28.1 us -> 27.5 us
    sub x1, other arithmetic: 1.32 us -> 0.61 us  [on_device(): return (latent + leap_step * half, half - 0.5 * leap_step * end_grad)]
    pallas_call x1, Pallas kernels: 28.1 us -> 27.5 us  [on_device(): pl.pallas_call(functools.partial(kernel, ngrp, ntile), out_shape=[pltpu.V...]
where the time goes in v4:
time: 28.9 us; the launch traced here: 28.7 us
  Pallas kernels  27.5 us (95%)
  between operations  0.66 us (2%)
  other arithmetic  0.61 us (2%)
    pallas_call x1, Pallas kernels, on_device(): pl.pallas_call(functools.partial(kernel, ngrp, ntile), out_shape=[pltpu.V...  27.5 us
    sub x1, other arithmetic, on_device(): return (latent + leap_step * half, half - 0.5 * leap_step * end_grad)  0.61 us

profile of v4, /device:TPU:0, one launch (start us, length us, event | category | flops | bytes accessed | tf_op | source)
XLA Modules:
  0.0 28.7 jit_solution(9030015257482895067)
XLA Ops:
  0.6 0.0 copy-start
  0.6 27.5 %shard_map.95 = (f32[16,128]{1,0:T(8,128)S(1)}, f32[16,128]{1,0:T(8,128)S(1)}) custom-call(f32[16,128]{1,0:T(8,128)} %latent_hbm.1, f32[16,128]{1,0:T(8,128)} %momentum_hbm.1, f32[16,128]{1,0:T(8,128)} %observed_hbm.1, f32[16,128]{1,0:T(8,128)} %nugget_hbm.1, f32[16,128,256]{2,1,0:T(8,128)} %cond_hbm.1, f32[16,128,128]{2,1,0:T(8,128)} %whiten_hbm.1, ...), custom_call_target="tpu_custom_call" | custom-call | tf_op jit(solution)/shard_map/pallas_call | solution.py:327
  28.1 0.0 copy-done
  28.1 0.6 %multiply_subtract_fusion = (f32[16,128]{1,0:T(8,128)}, f32[16,128]{1,0:T(8,128)}) fusion(f32[16,128]{1,0:T(8,128)S(1)} %get-tuple-element.4, f32[16,128]{1,0:T(8,128)S(1)} %get-tuple-element.5, f32[16,128]{1,0:T(8,128)S(1)} %copy-done), kind=kLoop, calls=%fused_computation | loop fusion | flops 8192 | bytes 40960 | tf_op jit(solution)/shard_map/sub | solution.py:358
Async XLA Ops:
  0.6 27.5 %copy-start = (f32[16,128]{1,0:T(8,128)S(1)}, f32[16,128]{1,0:T(8,128)}, u32[]{:S(2)}) copy-start(f32[16,128]{1,0:T(8,128)} %latent_hbm.1) | copy-start | bytes 24580

commit v5 on v4

--- a/solution.py
+++ b/solution.py
@@ -153,7 +153,9 @@
             sends.append(copy)
         return sends
 
-    def give(turn):
+    def give(turn, split):
+        sent[turn - 2, :halo] = jnp.dot(hot[:halo], split, preferred_element_type=jnp.float32)
+
         def send(flat, to):
             pltpu.make_async_remote_copy(
                 src_ref=sent.at[turn - 2, pl.ds(pl.multiple_of(flat * ROWS, ROWS), COARSE_DEV)],
@@ -165,6 +167,7 @@
             ).start()
 
         everyone(send)
+        sent[turn - 2, halo:] = jnp.dot(hot[halo:], split, preferred_element_type=jnp.float32)
         sends = []
         for side, (to, row) in enumerate(((above, halo + 2 * blocks), (below, halo))):
             copy = pltpu.make_async_remote_copy(
@@ -270,9 +273,7 @@
             piece = rest.astype(jnp.bfloat16)
             split.append(piece)
             rest = rest - piece.astype(jnp.float32)
-        sent[turn] = jnp.dot(
-            hot, jnp.concatenate(split, axis=0), preferred_element_type=jnp.float32
-        )
+        return jnp.concatenate(split, axis=0)
 
     def pulled_coarse(turn):
         total = landed[turn].reshape(devices, ROWS, width).sum(axis=0)
@@ -287,8 +288,7 @@
 
     arrive_near(first)
     arrive_coarse(0, table.at[0])
-    pushes(0, latent)
-    second = give(2)
+    second = give(2, pushes(0, latent))
     known = own[...] + (latent - observed_ref[...]) / nugget_ref[...]
     arrive_near(second)
     half = momentum_ref[...] - 0.5 * leap_step * (known - pulled_near(0))
@@ -303,8 +303,7 @@
     keep(1, moved)
     arrive_near(third)
     arrive_coarse(1, table.at[1])
-    pushes(1, moved)
-    fourth = give(3)
+    fourth = give(3, pushes(1, moved))
     known = own[...] + (moved - observed_ref[...]) / nugget_ref[...]
     arrive_near(fourth)
     known = known - pulled_near(1)

time: 28.9 us -> 28.8 us (level)
  no operation moved by 1% of the time
where the time goes in v5:
time: 28.8 us; the launch traced here: 28.6 us
  Pallas kernels  27.4 us (95%)
  between operations  0.66 us (2%)
  other arithmetic  0.61 us (2%)
    pallas_call x1, Pallas kernels, on_device(): pl.pallas_call(functools.partial(kernel, ngrp, ntile), out_shape=[pltpu.V...  27.4 us
    sub x1, other arithmetic, on_device(): return (latent + leap_step * half, half - 0.5 * leap_step * end_grad)  0.61 us

profile of v5, /device:TPU:0, one launch (start us, length us, event | category | flops | bytes accessed | tf_op | source)
XLA Modules:
  0.0 28.6 jit_solution(8089919170242410138)
XLA Ops:
  0.6 0.0 copy-start
  0.6 27.4 %shard_map.95 = (f32[16,128]{1,0:T(8,128)S(1)}, f32[16,128]{1,0:T(8,128)S(1)}) custom-call(f32[16,128]{1,0:T(8,128)} %latent_hbm.1, f32[16,128]{1,0:T(8,128)} %momentum_hbm.1, f32[16,128]{1,0:T(8,128)} %observed_hbm.1, f32[16,128]{1,0:T(8,128)} %nugget_hbm.1, f32[16,128,256]{2,1,0:T(8,128)} %cond_hbm.1, f32[16,128,128]{2,1,0:T(8,128)} %whiten_hbm.1, ...), custom_call_target="tpu_custom_call" | custom-call | tf_op jit(solution)/shard_map/pallas_call | solution.py:326
  28.0 0.0 copy-done
  28.0 0.6 %multiply_subtract_fusion = (f32[16,128]{1,0:T(8,128)}, f32[16,128]{1,0:T(8,128)}) fusion(f32[16,128]{1,0:T(8,128)S(1)} %get-tuple-element.4, f32[16,128]{1,0:T(8,128)S(1)} %get-tuple-element.5, f32[16,128]{1,0:T(8,128)S(1)} %copy-done), kind=kLoop, calls=%fused_computation | loop fusion | flops 8192 | bytes 40960 | tf_op jit(solution)/shard_map/sub | solution.py:357
Async XLA Ops:
  0.6 27.4 %copy-start = (f32[16,128]{1,0:T(8,128)S(1)}, f32[16,128]{1,0:T(8,128)}, u32[]{:S(2)}) copy-start(f32[16,128]{1,0:T(8,128)} %latent_hbm.1) | copy-start | bytes 24580
